TPU v7x, 32 devices: a whole 2x2x4 slice. The times are simulated.
32 devices in a mesh: region: 16 (over z, y, x), blk: 2 (over core).
Axes of the slice: x: 2, y: 2, z: 4, core: 2. Of those that a mesh axis runs over, the one named last changes fastest.
Arguments:
- site_tensors: float32 [128, 2, 32, 1024], P('region', 'blk'), may hold values from -18 to 18
- projectors: bfloat16 [128, 2, 32, 1024], P('region'), may hold values from -0.1875 to 0.1875
- gate_matrix: float32 [2, 2, 2, 2], replicated, may hold values from -3 to 3
- recv_src: int32 [128, 3], P('region'), may hold values from 0 to 88, as said below
- cut_list: int32 [160], P('region'), may hold values from 0 to 23, as said below
- cut_dest: int32 [16, 10], replicated, may hold values from -1 to 63, as said below
- gate_src: int32 [128], P('region'), may hold values from 0 to 24, as said below
- gate_list: int32 [32], P('region'), may hold values from 0 to 7, as said below
- gate_dest: int32 [16, 2], replicated, may hold values from -1 to 15, as said below
Outputs:
- new_sites: float32 [128, 2, 32, 1024], P('region', 'blk')
- messages: float32 [128, 3, 1024], P('region')
Inputs may be any that keep to these rules, and one draw needn't show every extreme that they name: `recv_src`: messages between one ordered pair of regions use distinct slots below 4; some pair uses all 4. `cut_list`: entries whose cut_dest is -1 are padding. `cut_dest`: some region fills all 10 entries of its row. `gate_src`: gate partners form pairs along vertical links. `gate_list`: entries whose gate_dest is -1 are padding. `gate_dest`: some region fills all 2 entries of its row.
All inputs are finite; a program needn't handle non-finite values.
Results may differ from a plain program's by a relative error of at most 0.0039.
Values may be sent and summed in bfloat16 or wider, within the bound.
A program may use at most 128 MiB of HBM per device.

v0:
```python
import jax
import jax.numpy as jnp
from jax import lax
from jax.sharding import PartitionSpec as P

SWEEPS = 2
CAP = 4
GCAP = 1
HIGHEST = lax.Precision.HIGHEST
EPSILON = 1e-06


def weighted(tensors, incoming):
    partial_a = jnp.einsum("isabc,iag->isgbc", tensors, incoming[:, 0], precision=HIGHEST)
    return jnp.einsum("isgbc,ibe->isgec", partial_a, incoming[:, 1], precision=HIGHEST)


def outgoing(tensors, incoming):
    partial_c = jnp.einsum("isabc,icd->isabd", tensors, incoming[:, 2], precision=HIGHEST)
    both_bc = jnp.einsum("isabd,ibe->isaed", partial_c, incoming[:, 1], precision=HIGHEST)
    leg_zero = jnp.einsum("isaed,isfed->iaf", both_bc, tensors, precision=HIGHEST)
    both_ac = jnp.einsum("isabd,iag->isgbd", partial_c, incoming[:, 0], precision=HIGHEST)
    leg_one = jnp.einsum("isgbd,isghd->ibh", both_ac, tensors, precision=HIGHEST)
    both_ab = weighted(tensors, incoming)
    leg_two = jnp.einsum("isgec,isgek->ick", both_ab, tensors, precision=HIGHEST)
    return jnp.stack([leg_zero, leg_one, leg_two], axis=1)


def normalized(leg_terms):
    trace_sum = jnp.trace(leg_terms, axis1=2, axis2=3)
    return leg_terms.shape[-1] * leg_terms / trace_sum[:, :, None, None]


def select_rows(dest_table, my_region, capacity):
    region_count, columns = dest_table.shape
    wanted = my_region * capacity + jnp.arange(capacity, dtype=jnp.int32)
    matched = dest_table[:, :, None] == wanted[None, None, :]
    position = jnp.sum(
        jnp.where(matched, jnp.arange(columns, dtype=jnp.int32)[None, :, None], 0), axis=1
    )
    return (jnp.arange(region_count, dtype=jnp.int32)[:, None] * columns + position).reshape(-1)


def shards(
    site_tensors,
    projectors,
    gate_matrix,
    recv_src,
    cut_list,
    cut_dest,
    gate_src,
    gate_list,
    gate_dest,
):
    site_count = site_tensors.shape[0]
    bond_dim = site_tensors.shape[2]
    regions = lax.axis_size("region")
    my_region = lax.axis_index("region")
    my_spin = lax.axis_index("blk")
    tensors = site_tensors.reshape(site_count, 1, bond_dim, bond_dim, bond_dim)
    boundary = jnp.zeros((bond_dim, bond_dim), jnp.float32).at[0, 0].set(bond_dim)
    identity = jnp.eye(bond_dim, dtype=jnp.float32)
    msg_none = 3 * site_count + regions * CAP
    incoming = jnp.where((recv_src == msg_none)[:, :, None, None], boundary, identity)
    edge_row = boundary.reshape(1, bond_dim * bond_dim)
    for sweep_index in range(SWEEPS):
        totals = lax.psum(outgoing(tensors, incoming), "blk")
        fresh_msgs = normalized(totals).reshape(3 * site_count, bond_dim * bond_dim)
        leaving = fresh_msgs[cut_list]
        everyone = lax.all_gather(leaving, "region", axis=0, tiled=True)
        arrived = everyone[select_rows(cut_dest, my_region, CAP)]
        lookup = jnp.concatenate([fresh_msgs, arrived, edge_row], axis=0)
        incoming = lookup[recv_src].reshape(site_count, 3, bond_dim, bond_dim)
    messages = incoming.reshape(site_count, 3, bond_dim * bond_dim)
    weights = (
        weighted(tensors, incoming)
        .astype(jnp.bfloat16)
        .reshape(site_count, bond_dim * bond_dim, bond_dim)
    )
    factor = jnp.einsum(
        "ikc,isnk->icsn", weights, projectors, preferred_element_type=jnp.float32
    ).astype(jnp.bfloat16)
    factor = factor.reshape(site_count, 1, bond_dim, 2 * bond_dim)
    halves = lax.all_gather(factor, "blk", axis=1, tiled=True)
    flat_factor = halves.reshape(site_count, 4 * bond_dim * bond_dim)
    leaving_factor = flat_factor[gate_list]
    everyone_factor = lax.all_gather(leaving_factor, "region", axis=0, tiled=True)
    arrived_factor = everyone_factor[select_rows(gate_dest, my_region, GCAP)]
    empty_row = jnp.zeros((1, 4 * bond_dim * bond_dim), jnp.bfloat16)
    factor_lookup = jnp.concatenate([flat_factor, arrived_factor, empty_row], axis=0)
    partners = factor_lookup[gate_src].reshape(site_count, 2, bond_dim, 2, bond_dim)
    mixing = jnp.einsum(
        "ajby,iycjn->iabcn", gate_matrix, partners.astype(jnp.float32), precision=HIGHEST
    )
    own_old = lax.dynamic_index_in_dim(mixing, my_spin, 2, keepdims=False)
    spin_piece = jnp.einsum("iuvc,iacn->iauvn", tensors[:, 0], own_old, precision=HIGHEST)
    spin_piece = spin_piece.reshape(site_count, 2, bond_dim, bond_dim * bond_dim)
    summed = lax.psum_scatter(spin_piece, "blk", scatter_dimension=1, tiled=True)
    squares = jnp.sum(summed * summed, axis=(1, 2, 3))
    total_sq = lax.psum(squares, "blk")
    mean_sq = total_sq / (2 * bond_dim**3)
    updated = summed / jnp.sqrt(mean_sq + EPSILON)[:, None, None, None]
    unchanged = gate_src == site_count + regions * GCAP
    new_sites = jnp.where(unchanged[:, None, None, None], site_tensors, updated)
    return (new_sites, messages)


def solution(mesh):
    return jax.shard_map(
        shards,
        mesh=mesh,
        in_specs=(
            P("region", "blk", None, None),
            P("region", None, None, None),
            P(),
            P("region", None),
            P("region"),
            P(),
            P("region"),
            P("region"),
            P(),
        ),
        out_specs=(P("region", "blk", None, None), P("region", None, None)),
        check_vma=False,
    )
```

profile of v0, /device:TPU:0, one launch (start us, length us, event | category | flops | bytes accessed | tf_op | source)
XLA Modules:
  0.0 483.6 jit_solution(1316465474755128273)
XLA Ops:
  7.2 0.8 broadcast_compare_fusion
  8.0 3.9 reshape.220
  11.9 6.4 %copy.94 = f32[8,32,32,32]{2,1,3,0:T(8,128)} copy(f32[8,32,32,32]{3,2,1,0:T(8,128)} %reshape.220) | data formatting | bytes 2097152 | tf_op jit(solution)/shard_map/reshape.47
  18.4 20.8 %convolution_bitcast_fusion.3 = f32[8,32,32,32]{2,3,1,0:T(8,128)S(1)} fusion(f32[8,32,32,32]{3,2,1,0:T(8,128)} %reshape.220, f32[8,3,32,32]{2,3,0,1:T(8,128)S(1)} %broadcast_select_fusion), kind=kOutput, calls=%fused_computation.35 | convolution fusion | flops 100663296 | bytes 2228224 | tf_op jit(solution)/shard_map/isabc,icd->isabd/dot_general | solution.py:19
  39.2 9.3 %fusion.14 = f32[8,32,32,32]{1,2,3,0:T(8,128)} fusion(f32[8,32,32,32]{2,3,1,0:T(8,128)S(1)} %convolution_bitcast_fusion.3, f32[8,3,32,32]{2,3,0,1:T(8,128)S(1)} %broadcast_select_fusion), kind=kOutput, calls=%fused_computation.23 | convolution fusion | flops 100663296 | bytes 5373952 | tf_op jit(solution)/shard_map/isabd,iag->isgbd/dot_general | solution.py:22
  48.5 20.6 %convolution_bitcast_fusion.2 = f32[8,32,32,32]{3,2,1,0:T(8,128)} fusion(f32[8,32,32,32]{2,3,1,0:T(8,128)S(1)} %convolution_bitcast_fusion.3, f32[8,3,32,32]{2,3,0,1:T(8,128)S(1)} %broadcast_select_fusion), kind=kOutput, calls=%fused_computation.34 | convolution fusion | flops 100663296 | bytes 5373952 | tf_op jit(solution)/shard_map/isabd,ibe->isaed/dot_general | solution.py:20
  69.1 6.8 %fusion.20 = f32[8,32,32,32]{3,1,2,0:T(8,128)} fusion(f32[8,32,32,32]{3,2,1,0:T(8,128)S(1)} %copy-done.1, f32[8,3,32,32]{2,3,0,1:T(8,128)S(1)} %broadcast_select_fusion), kind=kOutput, calls=%fused_computation.29 | convolution fusion | flops 100663296 | bytes 5373952 | tf_op jit(solution)/shard_map/isabc,iag->isgbc/dot_general | solution.py:14
  75.9 6.6 %copy.93 = f32[8,32,32,32]{2,1,3,0:T(8,128)} copy(f32[8,32,32,32]{3,2,1,0:T(8,128)} %convolution_bitcast_fusion.2) | data formatting | bytes 2097152 | tf_op jit(solution)/shard_map/reshape.51
  82.5 9.7 %convolution_bitcast_fusion.7 = f32[8,1,32,32]{3,2,0,1:T(8,128)S(1)} fusion(f32[8,32,32,32]{1,2,3,0:T(8,128)} %fusion.14, f32[8,32,32,32]{2,1,3,0:T(8,128)} %copy.94), kind=kOutput, calls=%fused_computation.43 | convolution fusion | flops 100663296 | bytes 2129920 | tf_op jit(solution)/shard_map/isgbd,isghd->ibh/dot_general | solution.py:23
  92.3 4.1 convolution_bitcast_fusion.8
  96.5 6.6 %fusion.12 = f32[8,32,32,32]{3,1,2,0:T(8,128)S(1)} fusion(f32[8,32,32,32]{3,1,2,0:T(8,128)S(1)} %copy-done.8, f32[8,3,32,32]{2,3,0,1:T(8,128)S(1)} %broadcast_select_fusion), kind=kOutput, calls=%fused_computation.21 | convolution fusion | flops 100663296 | bytes 5373952 | tf_op jit(solution)/shard_map/isgbc,ibe->isgec/dot_general | solution.py:15
  103.1 7.0 %fusion.28 = f32[8,1,32,32]{3,2,0,1:T(8,128)S(1)} fusion(f32[8,32,32,32]{3,2,1,0:T(8,128)S(1)} %copy-done.2, f32[8,32,32,32]{3,1,2,0:T(8,128)S(1)} %fusion.12), kind=kOutput, calls=%fused_computation.39 | convolution fusion | flops 100663296 | bytes 2129920 | tf_op jit(solution)/shard_map/isgec,isgek->ick/dot_general | solution.py:25
  110.2 0.8 pad_maximum_fusion.2
  111.1 2.7 reshape.344
  114.8 17.5 %all-reduce.5.cloned.1.call-done = f32[8,3,32,32]{3,2,0,1:T(8,128)} async-done(((f32[8,3,32,32]{3,2,0,1:T(8,128)}), f32[8,3,32,32]{3,2,0,1:T(8,128)}) %all-reduce.5.cloned.1.call-update) | async-done | bytes 98320 | tf_op jit(solution)/shard_map/psum | solution.py:67
  132.3 1.2 select_reduce_fusion.1
  133.4 1.1 multiply_divide_fusion.1
  135.3 49.6 %all-gather.3 = f32[16,10,1024]{2,1,0:T(8,128)} all-gather(f32[1,10,1024]{2,1,0:T(8,128)S(1)} %bitcast.197), channel_id=2, replica_groups=mesh['region'=16,'blk'=2] {'region'}, dimensions={0}, use_global_device_ids=true | all-gather | bytes 696320 | tf_op jit(solution)/shard_map/all_gather | solution.py:70
  185.0 1.3 reshape.320
  187.8 21.2 %convolution_bitcast_fusion.1 = f32[8,32,32,32]{2,3,1,0:T(8,128)S(1)} fusion(f32[8,32,32,32]{3,2,1,0:T(8,128)} %reshape.220, f32[8,3,32,32]{3,2,1,0:T(8,128)S(1)} %reshape.224), kind=kOutput, calls=%fused_computation.33 | convolution fusion | flops 100663296 | bytes 2228224 | tf_op jit(solution)/shard_map/isabc,icd->isabd/dot_general | solution.py:19
  209.0 8.4 %fusion.10 = f32[8,32,32,32]{1,2,3,0:T(8,128)S(1)} fusion(f32[8,32,32,32]{2,3,1,0:T(8,128)S(1)} %convolution_bitcast_fusion.1, f32[8,3,32,32]{3,2,1,0:T(8,128)S(1)} %reshape.224), kind=kOutput, calls=%fused_computation.19 | convolution fusion | flops 100663296 | bytes 5373952 | tf_op jit(solution)/shard_map/isabd,iag->isgbd/dot_general | solution.py:22
  217.4 21.1 %convolution_bitcast_fusion = f32[8,32,32,32]{3,2,1,0:T(8,128)} fusion(f32[8,32,32,32]{2,3,1,0:T(8,128)S(1)} %convolution_bitcast_fusion.1, f32[8,3,32,32]{3,2,1,0:T(8,128)S(1)} %reshape.224), kind=kOutput, calls=%fused_computation.32 | convolution fusion | flops 100663296 | bytes 5373952 | tf_op jit(solution)/shard_map/isabd,ibe->isaed/dot_general | solution.py:20
  238.5 6.9 %fusion.18 = f32[8,32,32,32]{3,1,2,0:T(8,128)} fusion(f32[8,32,32,32]{3,2,1,0:T(8,128)S(1)} %copy-done.3, f32[8,3,32,32]{3,2,1,0:T(8,128)S(1)} %reshape.224), kind=kOutput, calls=%fused_computation.27 | convolution fusion | flops 100663296 | bytes 5373952 | tf_op jit(solution)/shard_map/isabc,iag->isgbc/dot_general | solution.py:14
  245.4 6.3 %convolution_bitcast_fusion.5 = f32[8,1,32,32]{3,2,0,1:T(8,128)S(1)} fusion(f32[8,32,32,32]{1,2,3,0:T(8,128)S(1)} %fusion.10, f32[8,32,32,32]{2,1,3,0:T(8,128)S(1)} %copy-done.6), kind=kOutput, calls=%fused_computation.41 | convolution fusion | flops 100663296 | bytes 2129920 | tf_op jit(solution)/shard_map/isgbd,isghd->ibh/dot_general | solution.py:23
  251.7 6.5 %copy.109 = f32[8,32,32,32]{2,1,3,0:T(8,128)} copy(f32[8,32,32,32]{3,2,1,0:T(8,128)} %convolution_bitcast_fusion) | data formatting | bytes 2097152 | tf_op jit(solution)/shard_map/reshape.70
  258.2 7.7 %convolution_bitcast_fusion.6 = f32[8,1,32,32]{3,2,0,1:T(8,128)S(1)} fusion(f32[8,32,32,32]{2,1,3,0:T(8,128)} %copy.109, f32[8,32,32,32]{2,1,3,0:T(8,128)} %copy.94), kind=kOutput, calls=%fused_computation.42 | convolution fusion | flops 100663296 | bytes 2129920 | tf_op jit(solution)/shard_map/isaed,isfed->iaf/dot_general | solution.py:21
  266.0 6.2 %fusion.8 = f32[8,32,32,32]{3,1,2,0:T(8,128)S(1)} fusion(f32[8,32,32,32]{3,1,2,0:T(8,128)S(1)} %copy-done.7, f32[8,3,32,32]{3,2,1,0:T(8,128)S(1)} %reshape.224), kind=kOutput, calls=%fused_computation.17 | convolution fusion | flops 100663296 | bytes 5373952 | tf_op jit(solution)/shard_map/isgbc,ibe->isgec/dot_general | solution.py:15
  272.2 7.2 %fusion.31 = f32[8,1,32,32]{3,2,0,1:T(8,128)S(1)} fusion(f32[8,32,32,32]{3,2,1,0:T(8,128)S(1)} %copy-done.4, f32[8,32,32,32]{3,1,2,0:T(8,128)S(1)} %fusion.8), kind=kOutput, calls=%fused_computation.40 | convolution fusion | flops 100663296 | bytes 2129920 | tf_op jit(solution)/shard_map/isgec,isgek->ick/dot_general | solution.py:25
  279.4 0.8 pad_maximum_fusion.3
  280.2 14.5 %all-reduce.7.cloned.1.call-done = f32[8,3,32,32]{3,2,0,1:T(8,128)} async-done(((f32[8,3,32,32]{3,2,0,1:T(8,128)}), f32[8,3,32,32]{3,2,0,1:T(8,128)}) %all-reduce.7.cloned.1.call-update) | async-done | bytes 98320 | tf_op jit(solution)/shard_map/psum | solution.py:67
  294.7 1.2 select_reduce_fusion
  295.9 1.1 multiply_divide_fusion
  297.7 49.6 %all-gather.4 = f32[16,10,1024]{2,1,0:T(8,128)} all-gather(f32[1,10,1024]{2,1,0:T(8,128)S(1)} %bitcast.196), channel_id=3, replica_groups=mesh['region'=16,'blk'=2] {'region'}, dimensions={0}, use_global_device_ids=true | all-gather | bytes 696320 | tf_op jit(solution)/shard_map/all_gather | solution.py:70
  347.4 1.3 reshape.322
  350.1 8.3 %fusion.16 = f32[8,32,32,32]{3,1,2,0:T(8,128)S(1)} fusion(f32[8,32,32,32]{3,2,1,0:T(8,128)} %reshape.220, f32[8,3,32,32]{3,2,1,0:T(8,128)S(1)} %reshape.228), kind=kOutput, calls=%fused_computation.25 | convolution fusion | flops 100663296 | bytes 2228224 | tf_op jit(solution)/shard_map/isabc,iag->isgbc/dot_general | solution.py:14
  358.5 5.6 %fusion.25 = bf16[8,32,32,32]{3,1,2,0:T(8,128)(2,1)S(1)} fusion(f32[8,32,32,32]{3,1,2,0:T(8,128)S(1)} %fusion.16, f32[8,3,32,32]{3,2,1,0:T(8,128)S(1)} %reshape.228), kind=kOutput, calls=%fused_computation.36 | convolution fusion | flops 100925440 | bytes 4849664 | tf_op jit(solution)/shard_map/isgbc,ibe->isgec/dot_general | solution.py:15
  364.1 0.9 convolution_convert_fusion
  365.3 2.2 all_gather.14
  368.2 37.0 %all-gather.5 = bf16[16,2,4096]{2,1,0:T(2,128)(2,1)S(1)} all-gather(bf16[1,2,4096]{2,1,0:T(2,128)(2,1)S(1)} %bitcast.198), channel_id=4, replica_groups=mesh['region'=16,'blk'=2] {'region'}, dimensions={0}, use_global_device_ids=true | all-gather | bytes 278528 | tf_op jit(solution)/shard_map/all_gather | solution.py:87
  406.8 1.1 convolution_bitcast_fusion.4
  408.2 24.5 %fusion.22 = f32[8,2,32,32,32]{3,4,2,1,0:T(8,128)} fusion(f32[8,32,32,32,1]{3,2,1,0,4:T(8,128)} %reshape.344, f32[8,2,32,32,1]{3,1,2,0,4:T(2,128)S(1)} %bitcast.195), kind=kOutput, calls=%fused_computation.31 | convolution fusion | flops 201326592 | bytes 3211264 | tf_op jit(solution)/shard_map/iuvc,iacn->iauvn/dot_general | solution.py:96
  432.7 9.0 %copy.129 = f32[8,2,32,32,32]{4,3,2,1,0:T(8,128)} copy(f32[8,2,32,32,32]{3,4,2,1,0:T(8,128)} %fusion.22) | data formatting | bytes 4194304 | tf_op jit(solution)/shard_map/iuvc,iacn->iauvn/transpose | solution.py:96
  441.6 7.7 %reshape.233 = f32[8,2,32,1024]{3,2,1,0:T(8,128)} reshape(f32[8,2,32,32,32]{4,3,2,1,0:T(8,128)} %copy.129) | data formatting | bytes 4194304 | tf_op jit(solution)/shard_map/reshape | solution.py:97
  450.0 18.5 %all-reduce.9.cloned.1.call-done = f32[8,2,32,1024]{3,2,1,0:T(8,128)} async-done(((f32[8,2,32,1024]{3,2,1,0:T(8,128)}), f32[8,2,32,1024]{3,2,1,0:T(8,128)}) %all-reduce.9.cloned.1.call-update) | async-done | bytes 2097168
  468.5 2.0 multiply_reduce_fusion
  470.5 0.7 copy.130
  471.2 2.4 psum.23
  473.6 3.0 divide_select_fusion
  (105 shorter events, 9.2 us)
Async XLA Ops:
  7.2 356.9 %copy-start = (bf16[8,2,32,1024]{3,2,1,0:T(8,128)(2,1)S(1)}, bf16[8,2,32,1024]{3,2,1,0:T(8,128)(2,1)}, u32[]{:S(2)}) copy-start(bf16[8,2,32,1024]{3,2,1,0:T(8,128)(2,1)} %param.12) | copy-start | bytes 3145732
  7.2 125.1 %all-reduce.5.cloned.1.call-start = ((), (), s32[]{:S(2)}) async-start(), calls=%async_computation | async-start | bytes 786432 | tf_op jit(solution)/shard_map/psum | solution.py:67
  11.9 6.4 %copy-start.12 = (f32[32,32]{0,1:T(8,128)S(1)}, f32[32,32]{0,1:T(8,128)}, u32[]{:S(2)}) copy-start(f32[32,32]{0,1:T(8,128)} %constant.75.clone.1) | copy-start | bytes 12292
  48.5 20.6 %copy-start.1 = (f32[8,32,32,32]{3,2,1,0:T(8,128)S(1)}, f32[8,32,32,32]{3,2,1,0:T(8,128)}, u32[]{:S(2)}) copy-start(f32[8,32,32,32]{3,2,1,0:T(8,128)} %reshape.220) | copy-start | bytes 3145732
  82.5 9.8 %copy-start.5 = (f32[8,32,32,32]{2,1,3,0:T(8,128)S(1)}, f32[8,32,32,32]{2,1,3,0:T(8,128)}, u32[]{:S(2)}) copy-start(f32[8,32,32,32]{2,1,3,0:T(8,128)} %copy.94) | copy-start | bytes 3145732
  82.5 9.8 %copy-start.9 = (f32[8,32,32,32]{2,1,3,0:T(8,128)S(1)}, f32[8,32,32,32]{2,1,3,0:T(8,128)}, u32[]{:S(2)}) copy-start(f32[8,32,32,32]{2,1,3,0:T(8,128)} %copy.93) | copy-start | bytes 3145732
  92.3 4.1 copy-start.8
  96.4 6.6 %copy-start.2 = (f32[8,32,32,32]{3,2,1,0:T(8,128)S(1)}, f32[8,32,32,32]{3,2,1,0:T(8,128)}, u32[]{:S(2)}) copy-start(f32[8,32,32,32]{3,2,1,0:T(8,128)} %reshape.220) | copy-start | bytes 3145732
  103.1 7.9 %copy-start.13 = (s32[8,3]{0,1:T(4,128)S(1)}, s32[8,3]{0,1:T(4,128)}, u32[]{:S(2)}) copy-start(s32[8,3]{0,1:T(4,128)} %param.14) | copy-start | bytes 292
  103.1 8.0 %copy-start.10 = (f32[8,1,32,1024]{3,2,1,0:T(8,128)S(1)}, f32[8,1,32,1024]{3,2,1,0:T(8,128)}, u32[]{:S(2)}) copy-start(f32[8,1,32,1024]{3,2,1,0:T(8,128)} %param.11) | copy-start | bytes 3145732
  110.1 3.7 copy-start.16
  110.1 3.7 copy-start.17
  110.1 3.8 copy-start.18
  110.1 3.8 copy-start.19
  110.1 4.0 copy-start.15
  110.1 4.2 copy-start.14
  111.0 183.7 %all-reduce.7.cloned.1.call-start = ((), (), s32[]{:S(2)}) async-start(), calls=%async_computation.1 | async-start | bytes 786432 | tf_op jit(solution)/shard_map/psum | solution.py:67
  113.8 73.2 %copy-start.11 = (f32[1,1024]{1,0:T(1,128)S(1)}, f32[1,1024]{1,0:T(1,128)}, u32[]{:S(2)}) copy-start(f32[1,1024]{1,0:T(1,128)} %constant.84.clone.1) | copy-start | bytes 12292
  217.4 21.2 %copy-start.3 = (f32[8,32,32,32]{3,2,1,0:T(8,128)S(1)}, f32[8,32,32,32]{3,2,1,0:T(8,128)}, u32[]{:S(2)}) copy-start(f32[8,32,32,32]{3,2,1,0:T(8,128)} %reshape.220) | copy-start | bytes 3145732
  238.5 6.9 %copy-start.6 = (f32[8,32,32,32]{2,1,3,0:T(8,128)S(1)}, f32[8,32,32,32]{2,1,3,0:T(8,128)}, u32[]{:S(2)}) copy-start(f32[8,32,32,32]{2,1,3,0:T(8,128)} %copy.94) | copy-start | bytes 3145732
  258.2 7.7 %copy-start.7 = (f32[8,32,32,32]{3,1,2,0:T(8,128)S(1)}, f32[8,32,32,32]{3,1,2,0:T(8,128)}, u32[]{:S(2)}) copy-start(f32[8,32,32,32]{3,1,2,0:T(8,128)} %fusion.18) | copy-start | bytes 3145732
  266.0 6.2 %copy-start.4 = (f32[8,32,32,32]{3,2,1,0:T(8,128)S(1)}, f32[8,32,32,32]{3,2,1,0:T(8,128)}, u32[]{:S(2)}) copy-start(f32[8,32,32,32]{3,2,1,0:T(8,128)} %reshape.220) | copy-start | bytes 3145732
  280.2 188.3 %all-reduce.9.cloned.1.call-start = ((), (), s32[]{:S(2)}) async-start(), calls=%async_computation.2 | async-start | bytes 4194304
  441.6 7.7 %copy-start.20 = (u32[32]{0:T(128)S(1)}, u32[32]{0:T(128)}, u32[]{:S(2)}) copy-start(u32[32]{0:T(128)} %constant.101) | copy-start | bytes 388
Sparse Core Ops, SparseCore 0:
  111.1 21.1 all-reduce.4
  280.3 14.3 all-reduce.6
  449.5 19.0 all-reduce.8
where the time goes:
time: 492 us; the launch traced here: 484 us
  matrix products  210 us (43%)
  blocking collectives  141 us (29%)
  local copies, waits for them, and re-layouts  54.7 us (11%)
  waiting for transfers between devices  50.5 us (10%)
  between operations  14.8 us (3%)
  other arithmetic  12.3 us (2%)
    all_gather x2, blocking collectives, shards(): everyone = lax.all_gather(leaving, 'region', axis=0, tiled=True)  99.2 us
    dot_general x2, matrix products, outgoing(): jnp.einsum('isabc,icd->isabd', tensors, incoming[:, 2], precision=HIGHEST)  42 us
    dot_general x2, matrix products, outgoing(): jnp.einsum('isabd,ibe->isaed', partial_c, incoming[:, 1], precision=HIGHEST)  41.8 us
    all_gather x1, blocking collectives, shards(): lax.all_gather(leaving_factor, 'region', axis=0, tiled=True)  37 us
    psum x2, waiting for transfers between devices, shards(): totals = lax.psum(outgoing(tensors, incoming), 'blk')  32 us
    another operation x6, local copies, waits for them, and re-layouts  26.4 us
    dot_general x1, matrix products, shards(): jnp.einsum('iuvc,iacn->iauvn', tensors[:, 0], own_old, precision=HIGHEST)  24.5 us
    dot_general x3, matrix products, weighted(): jnp.einsum('isabc,iag->isgbc', tensors, incoming[:, 0], precision=HIGHEST)  22.1 us
  transfers between devices with their start and end apart: 3, of which 3 were waited for; matrix products, arithmetic and copies ran while one was open for 1% of the time, Pallas kernels for 0%

commit v1 on v0

--- a/solution.py
+++ b/solution.py
@@ -64,7 +64,7 @@
     incoming = jnp.where((recv_src == msg_none)[:, :, None, None], boundary, identity)
     edge_row = boundary.reshape(1, bond_dim * bond_dim)
     for sweep_index in range(SWEEPS):
-        totals = lax.psum(outgoing(tensors, incoming), "blk")
+        totals = jnp.sum(lax.all_gather(outgoing(tensors, incoming), "blk"), axis=0)
         fresh_msgs = normalized(totals).reshape(3 * site_count, bond_dim * bond_dim)
         leaving = fresh_msgs[cut_list]
         everyone = lax.all_gather(leaving, "region", axis=0, tiled=True)

time: 492 us -> 463 us (0.941)
  waiting for transfers between devices: 50.5 us -> 16.5 us
  matrix products: 210 us -> 215 us
    psum x2 -> x0, waiting for transfers between devices: 32 us -> none  [shards(): totals = lax.psum(outgoing(tensors, incoming), 'blk')]
    all_gather x2, blocking collectives: 99.2 us -> 92.8 us  [shards(): everyone = lax.all_gather(leaving, 'region', axis=0, tiled=True)]
    unnamed x4 -> x2, waiting for transfers between devices: 18.6 us -> 16.5 us
  transfers between devices with their start and end apart: 3 -> 1, of which waited for: 3 -> 1; matrix products, arithmetic and copies ran while one was open for 1% -> 0% of each run, Pallas kernels for 0% -> 0%
where the time goes in v1:
time: 463 us; the launch traced here: 454 us
  matrix products  215 us (46%)
  blocking collectives  141 us (30%)
  local copies, waits for them, and re-layouts  55.2 us (12%)
  waiting for transfers between devices  16.5 us (4%)
  between operations  15 us (3%)
  other arithmetic  11.3 us (2%)
    all_gather x2, blocking collectives, shards(): everyone = lax.all_gather(leaving, 'region', axis=0, tiled=True)  92.8 us
    dot_general x2, matrix products, outgoing(): jnp.einsum('isabc,icd->isabd', tensors, incoming[:, 2], precision=HIGHEST)  42 us
    dot_general x2, matrix products, outgoing(): jnp.einsum('isabd,ibe->isaed', partial_c, incoming[:, 1], precision=HIGHEST)  41.8 us
    all_gather x1, blocking collectives, shards(): lax.all_gather(leaving_factor, 'region', axis=0, tiled=True)  39.2 us
    another operation x6, local copies, waits for them, and re-layouts  26.6 us
    dot_general x1, matrix products, shards(): jnp.einsum('iuvc,iacn->iauvn', tensors[:, 0], own_old, precision=HIGHEST)  24.5 us
    dot_general x3, matrix products, weighted(): jnp.einsum('isabc,iag->isgbc', tensors, incoming[:, 0], precision=HIGHEST)  22.1 us
    dot_general x2, matrix products, outgoing(): jnp.einsum('isgbd,isghd->ibh', both_ac, tensors, precision=HIGHEST)  19.5 us
  transfers between devices with their start and end apart: 1, of which 1 were waited for; matrix products, arithmetic and copies ran while one was open for 0% of the time, Pallas kernels for 0%

profile of v1, /device:TPU:0, one launch (start us, length us, event | category | flops | bytes accessed | tf_op | source)
XLA Modules:
  0.0 454.2 jit_solution(2003061511765591170)
XLA Ops:
  7.2 0.8 broadcast_compare_fusion
  8.7 3.9 reshape.226
  12.6 6.4 %copy.131 = f32[8,32,32,32]{2,1,3,0:T(8,128)} copy(f32[8,32,32,32]{3,2,1,0:T(8,128)} %reshape.226) | data formatting | bytes 2097152 | tf_op jit(solution)/shard_map/reshape.47
  19.1 20.8 %convolution_bitcast_fusion.3 = f32[8,32,32,32]{2,3,1,0:T(8,128)S(1)} fusion(f32[8,32,32,32]{3,2,1,0:T(8,128)} %reshape.226, f32[8,3,32,32]{2,3,0,1:T(8,128)S(1)} %broadcast_select_fusion), kind=kOutput, calls=%fused_computation.35 | convolution fusion | flops 100663296 | bytes 2228224 | tf_op jit(solution)/shard_map/isabc,icd->isabd/dot_general | solution.py:19
  39.9 9.3 %fusion.14 = f32[8,32,32,32]{1,2,3,0:T(8,128)} fusion(f32[8,32,32,32]{2,3,1,0:T(8,128)S(1)} %convolution_bitcast_fusion.3, f32[8,3,32,32]{2,3,0,1:T(8,128)S(1)} %broadcast_select_fusion), kind=kOutput, calls=%fused_computation.23 | convolution fusion | flops 100663296 | bytes 5373952 | tf_op jit(solution)/shard_map/isabd,iag->isgbd/dot_general | solution.py:22
  49.2 20.7 %convolution_bitcast_fusion.2 = f32[8,32,32,32]{3,2,1,0:T(8,128)} fusion(f32[8,32,32,32]{2,3,1,0:T(8,128)S(1)} %convolution_bitcast_fusion.3, f32[8,3,32,32]{2,3,0,1:T(8,128)S(1)} %broadcast_select_fusion), kind=kOutput, calls=%fused_computation.34 | convolution fusion | flops 100663296 | bytes 5373952 | tf_op jit(solution)/shard_map/isabd,ibe->isaed/dot_general | solution.py:20
  69.9 6.8 %fusion.20 = f32[8,32,32,32]{3,1,2,0:T(8,128)} fusion(f32[8,32,32,32]{3,2,1,0:T(8,128)S(1)} %copy-done.1, f32[8,3,32,32]{2,3,0,1:T(8,128)S(1)} %broadcast_select_fusion), kind=kOutput, calls=%fused_computation.29 | convolution fusion | flops 100663296 | bytes 5373952 | tf_op jit(solution)/shard_map/isabc,iag->isgbc/dot_general | solution.py:14
  77.4 6.8 %copy.130 = f32[8,32,32,32]{2,1,3,0:T(8,128)} copy(f32[8,32,32,32]{3,2,1,0:T(8,128)} %convolution_bitcast_fusion.2) | data formatting | bytes 2097152 | tf_op jit(solution)/shard_map/reshape.51
  84.2 9.8 %convolution_bitcast_fusion.7 = f32[8,1,32,32]{3,2,0,1:T(8,128)S(1)} fusion(f32[8,32,32,32]{1,2,3,0:T(8,128)} %fusion.14, f32[8,32,32,32]{2,1,3,0:T(8,128)} %copy.131), kind=kOutput, calls=%fused_computation.43 | convolution fusion | flops 100663296 | bytes 2129920 | tf_op jit(solution)/shard_map/isgbd,isghd->ibh/dot_general | solution.py:23
  94.1 4.1 convolution_bitcast_fusion.8
  98.2 6.3 %fusion.12 = f32[8,32,32,32]{3,1,2,0:T(8,128)S(1)} fusion(f32[8,32,32,32]{3,1,2,0:T(8,128)S(1)} %copy-done.6, f32[8,3,32,32]{2,3,0,1:T(8,128)S(1)} %broadcast_select_fusion), kind=kOutput, calls=%fused_computation.21 | convolution fusion | flops 100663296 | bytes 5373952 | tf_op jit(solution)/shard_map/isgbc,ibe->isgec/dot_general | solution.py:15
  104.5 7.0 %fusion.28 = f32[8,1,32,32]{3,2,0,1:T(8,128)S(1)} fusion(f32[8,32,32,32]{3,2,1,0:T(8,128)S(1)} %copy-done.2, f32[8,32,32,32]{3,1,2,0:T(8,128)S(1)} %fusion.12), kind=kOutput, calls=%fused_computation.39 | convolution fusion | flops 100663296 | bytes 2129920 | tf_op jit(solution)/shard_map/isgec,isgek->ick/dot_general | solution.py:25
  111.6 2.5 all-gather
  115.4 49.0 %all-gather.5 = f32[16,10,1024]{2,1,0:T(8,128)S(1)} all-gather(f32[1,10,1024]{2,1,0:T(8,128)S(1)} %bitcast.201), channel_id=3, replica_groups=mesh['region'=16,'blk'=2] {'region'}, dimensions={0}, use_global_device_ids=true | all-gather | bytes 696320 | tf_op jit(solution)/shard_map/all_gather | solution.py:70
  165.9 21.3 %convolution_bitcast_fusion.1 = f32[8,32,32,32]{2,3,1,0:T(8,128)S(1)} fusion(f32[8,32,32,32]{3,2,1,0:T(8,128)} %reshape.226, f32[8,3,32,32]{3,2,1,0:T(8,128)S(1)} %reshape.229), kind=kOutput, calls=%fused_computation.33 | convolution fusion | flops 100663296 | bytes 2228224 | tf_op jit(solution)/shard_map/isabc,icd->isabd/dot_general | solution.py:19
  187.2 9.3 %fusion.10 = f32[8,32,32,32]{1,2,3,0:T(8,128)} fusion(f32[8,32,32,32]{2,3,1,0:T(8,128)S(1)} %convolution_bitcast_fusion.1, f32[8,3,32,32]{3,2,1,0:T(8,128)S(1)} %reshape.229), kind=kOutput, calls=%fused_computation.19 | convolution fusion | flops 100663296 | bytes 5373952 | tf_op jit(solution)/shard_map/isabd,iag->isgbd/dot_general | solution.py:22
  196.5 21.1 %convolution_bitcast_fusion = f32[8,32,32,32]{3,2,1,0:T(8,128)} fusion(f32[8,32,32,32]{2,3,1,0:T(8,128)S(1)} %convolution_bitcast_fusion.1, f32[8,3,32,32]{3,2,1,0:T(8,128)S(1)} %reshape.229), kind=kOutput, calls=%fused_computation.32 | convolution fusion | flops 100663296 | bytes 5373952 | tf_op jit(solution)/shard_map/isabd,ibe->isaed/dot_general | solution.py:20
  217.6 6.9 %fusion.18 = f32[8,32,32,32]{3,1,2,0:T(8,128)} fusion(f32[8,32,32,32]{3,2,1,0:T(8,128)S(1)} %copy-done.3, f32[8,3,32,32]{3,2,1,0:T(8,128)S(1)} %reshape.229), kind=kOutput, calls=%fused_computation.27 | convolution fusion | flops 100663296 | bytes 5373952 | tf_op jit(solution)/shard_map/isabc,iag->isgbc/dot_general | solution.py:14
  224.6 2.7 reshape.350
  229.2 0.7 copy.192
  229.9 9.7 %convolution_bitcast_fusion.5 = f32[8,1,32,32]{3,2,0,1:T(8,128)S(1)} fusion(f32[8,32,32,32]{1,2,3,0:T(8,128)} %fusion.10, f32[8,32,32,32]{2,1,3,0:T(8,128)} %copy.131), kind=kOutput, calls=%fused_computation.41 | convolution fusion | flops 100663296 | bytes 2129920 | tf_op jit(solution)/shard_map/isgbd,isghd->ibh/dot_general | solution.py:23
  239.6 6.5 %copy.147 = f32[8,32,32,32]{2,1,3,0:T(8,128)} copy(f32[8,32,32,32]{3,2,1,0:T(8,128)} %convolution_bitcast_fusion) | data formatting | bytes 2097152 | tf_op jit(solution)/shard_map/reshape.70
  246.1 7.7 %convolution_bitcast_fusion.6 = f32[8,1,32,32]{3,2,0,1:T(8,128)S(1)} fusion(f32[8,32,32,32]{2,1,3,0:T(8,128)} %copy.147, f32[8,32,32,32]{2,1,3,0:T(8,128)} %copy.131), kind=kOutput, calls=%fused_computation.42 | convolution fusion | flops 100663296 | bytes 2129920 | tf_op jit(solution)/shard_map/isaed,isfed->iaf/dot_general | solution.py:21
  253.8 6.2 %fusion.8 = f32[8,32,32,32]{3,1,2,0:T(8,128)S(1)} fusion(f32[8,32,32,32]{3,1,2,0:T(8,128)S(1)} %copy-done.7, f32[8,3,32,32]{3,2,1,0:T(8,128)S(1)} %reshape.229), kind=kOutput, calls=%fused_computation.17 | convolution fusion | flops 100663296 | bytes 5373952 | tf_op jit(solution)/shard_map/isgbc,ibe->isgec/dot_general | solution.py:15
  260.0 7.2 %fusion.31 = f32[8,1,32,32]{3,2,0,1:T(8,128)S(1)} fusion(f32[8,32,32,32]{3,2,1,0:T(8,128)S(1)} %copy-done.4, f32[8,32,32,32]{3,1,2,0:T(8,128)S(1)} %fusion.8), kind=kOutput, calls=%fused_computation.40 | convolution fusion | flops 100663296 | bytes 2129920 | tf_op jit(solution)/shard_map/isgec,isgek->ick/dot_general | solution.py:25
  267.3 2.4 all-gather.2
  269.6 0.8 reduce_sum.70
  270.5 1.2 select_reduce_fusion
  272.1 0.7 gather_fusion.3
  272.8 43.8 %all-gather.6 = f32[16,10,1024]{2,1,0:T(8,128)} all-gather(f32[1,10,1024]{2,1,0:T(8,128)S(1)} %bitcast.200), channel_id=5, replica_groups=mesh['region'=16,'blk'=2] {'region'}, dimensions={0}, use_global_device_ids=true | all-gather | bytes 696320 | tf_op jit(solution)/shard_map/all_gather | solution.py:70
  316.6 1.3 reshape.328
  319.4 8.3 %fusion.16 = f32[8,32,32,32]{3,1,2,0:T(8,128)S(1)} fusion(f32[8,32,32,32]{3,2,1,0:T(8,128)} %reshape.226, f32[8,3,32,32]{3,2,1,0:T(8,128)S(1)} %reshape.232), kind=kOutput, calls=%fused_computation.25 | convolution fusion | flops 100663296 | bytes 2228224 | tf_op jit(solution)/shard_map/isabc,iag->isgbc/dot_general | solution.py:14
  327.7 5.6 %fusion.25 = bf16[8,32,32,32]{3,1,2,0:T(8,128)(2,1)S(1)} fusion(f32[8,32,32,32]{3,1,2,0:T(8,128)S(1)} %fusion.16, f32[8,3,32,32]{3,2,1,0:T(8,128)S(1)} %reshape.232), kind=kOutput, calls=%fused_computation.36 | convolution fusion | flops 100925440 | bytes 4849664 | tf_op jit(solution)/shard_map/isgbc,ibe->isgec/dot_general | solution.py:15
  333.4 0.9 convolution_convert_fusion
  334.6 2.2 all_gather.30
  336.9 0.7 gather_fusion.6
  337.6 39.2 %all-gather.7 = bf16[16,2,4096]{2,1,0:T(2,128)(2,1)S(1)} all-gather(bf16[1,2,4096]{2,1,0:T(2,128)(2,1)S(1)} %bitcast.202), channel_id=6, replica_groups=mesh['region'=16,'blk'=2] {'region'}, dimensions={0}, use_global_device_ids=true | all-gather | bytes 278528 | tf_op jit(solution)/shard_map/all_gather | solution.py:87
  377.0 0.7 gather_fusion.7
  377.8 0.7 gather_fusion.8
  378.8 1.1 convolution_bitcast_fusion.4
  380.1 24.5 %fusion.22 = f32[8,2,32,32,32]{3,4,2,1,0:T(8,128)} fusion(f32[8,32,32,32,1]{3,2,1,0,4:T(8,128)} %reshape.350, f32[8,2,32,32,1]{3,1,2,0,4:T(2,128)S(1)} %bitcast.199), kind=kOutput, calls=%fused_computation.31 | convolution fusion | flops 201326592 | bytes 3211264 | tf_op jit(solution)/shard_map/iuvc,iacn->iauvn/dot_general | solution.py:96
  404.7 9.0 %copy.168 = f32[8,2,32,32,32]{4,3,2,1,0:T(8,128)} copy(f32[8,2,32,32,32]{3,4,2,1,0:T(8,128)} %fusion.22) | data formatting | bytes 4194304 | tf_op jit(solution)/shard_map/iuvc,iacn->iauvn/transpose | solution.py:96
  413.7 7.7 %reshape.237 = f32[8,2,32,1024]{3,2,1,0:T(8,128)} reshape(f32[8,2,32,32,32]{4,3,2,1,0:T(8,128)} %copy.168) | data formatting | bytes 4194304 | tf_op jit(solution)/shard_map/reshape | solution.py:97
  422.2 16.5 %all-reduce.3.cloned.1.call-done = f32[8,2,32,1024]{3,2,1,0:T(8,128)} async-done(((f32[8,2,32,1024]{3,2,1,0:T(8,128)}), f32[8,2,32,1024]{3,2,1,0:T(8,128)}) %all-reduce.3.cloned.1.call-update) | async-done | bytes 2097168
  438.7 2.0 multiply_reduce_fusion
  440.7 0.7 copy.169
  441.4 2.4 psum.7
  443.9 3.1 divide_select_fusion
  (109 shorter events, 10.1 us)
Async XLA Ops:
  7.2 326.2 %copy-start = (bf16[8,2,32,1024]{3,2,1,0:T(8,128)(2,1)S(1)}, bf16[8,2,32,1024]{3,2,1,0:T(8,128)(2,1)}, u32[]{:S(2)}) copy-start(bf16[8,2,32,1024]{3,2,1,0:T(8,128)(2,1)} %param.12) | copy-start | bytes 3145732
  7.2 431.5 %all-reduce.3.cloned.1.call-start = ((), (), s32[]{:S(2)}) async-start(), calls=%async_computation | async-start | bytes 4194304
  12.6 6.4 %copy-start.11 = (f32[32,32]{0,1:T(8,128)S(1)}, f32[32,32]{0,1:T(8,128)}, u32[]{:S(2)}) copy-start(f32[32,32]{0,1:T(8,128)} %constant.75.clone.1) | copy-start | bytes 12292
  49.2 20.7 %copy-start.1 = (f32[8,32,32,32]{3,2,1,0:T(8,128)S(1)}, f32[8,32,32,32]{3,2,1,0:T(8,128)}, u32[]{:S(2)}) copy-start(f32[8,32,32,32]{3,2,1,0:T(8,128)} %reshape.226) | copy-start | bytes 3145732
  69.9 6.8 %copy-start.17 = (s32[10]{0:T(128)S(1)}, s32[10]{0:T(128)}, u32[]{:S(2)}) copy-start(s32[10]{0:T(128)} %param.15) | copy-start | bytes 124
  69.9 7.1 %copy-start.12 = (s32[16,10]{1,0:T(8,128)S(1)}, s32[16,10]{1,0:T(8,128)}, u32[]{:S(2)}) copy-start(s32[16,10]{1,0:T(8,128)} %param.16) | copy-start | bytes 1924
  76.9 37.9 %copy-start.13 = (s32[1024]{0:T(1024)}, s32[1024]{0:T(1024)S(1)}, u32[]{:S(2)}) copy-start(s32[1024]{0:T(1024)S(1)} %pad_clamp_fusion.5) | copy-start | bytes 12292
  84.2 9.9 %copy-start.5 = (f32[8,32,32,32]{2,1,3,0:T(8,128)S(1)}, f32[8,32,32,32]{2,1,3,0:T(8,128)}, u32[]{:S(2)}) copy-start(f32[8,32,32,32]{2,1,3,0:T(8,128)} %copy.131) | copy-start | bytes 3145732
  84.2 9.9 %copy-start.8 = (f32[8,32,32,32]{2,1,3,0:T(8,128)S(1)}, f32[8,32,32,32]{2,1,3,0:T(8,128)}, u32[]{:S(2)}) copy-start(f32[8,32,32,32]{2,1,3,0:T(8,128)} %copy.130) | copy-start | bytes 3145732
  94.1 4.1 copy-start.6
  98.2 6.3 %copy-start.2 = (f32[8,32,32,32]{3,2,1,0:T(8,128)S(1)}, f32[8,32,32,32]{3,2,1,0:T(8,128)}, u32[]{:S(2)}) copy-start(f32[8,32,32,32]{3,2,1,0:T(8,128)} %reshape.226) | copy-start | bytes 3145732
  114.1 51.0 %copy-start.10 = (f32[1,1024]{1,0:T(1,128)S(1)}, f32[1,1024]{1,0:T(1,128)}, u32[]{:S(2)}) copy-start(f32[1,1024]{1,0:T(1,128)} %constant.84.clone.1) | copy-start | bytes 12292
  196.5 21.1 %copy-start.3 = (f32[8,32,32,32]{3,2,1,0:T(8,128)S(1)}, f32[8,32,32,32]{3,2,1,0:T(8,128)}, u32[]{:S(2)}) copy-start(f32[8,32,32,32]{3,2,1,0:T(8,128)} %reshape.226) | copy-start | bytes 3145732
  217.6 6.9 %copy-start.9 = (f32[8,1,32,1024]{3,2,1,0:T(8,128)S(1)}, f32[8,1,32,1024]{3,2,1,0:T(8,128)}, u32[]{:S(2)}) copy-start(f32[8,1,32,1024]{3,2,1,0:T(8,128)} %param.11) | copy-start | bytes 3145732
  224.6 2.7 copy-start.16
  224.6 2.8 copy-start.18
  224.6 2.8 copy-start.19
  224.6 4.6 %copy-start.14 = (f32[2,2,2,2]{3,2,1,0:T(2,128)S(1)}, f32[2,2,2,2]{3,2,1,0:T(2,128)}, u32[]{:S(2)}) copy-start(f32[2,2,2,2]{3,2,1,0:T(2,128)} %param.13) | copy-start | bytes 196
  246.1 7.7 %copy-start.7 = (f32[8,32,32,32]{3,1,2,0:T(8,128)S(1)}, f32[8,32,32,32]{3,1,2,0:T(8,128)}, u32[]{:S(2)}) copy-start(f32[8,32,32,32]{3,1,2,0:T(8,128)} %fusion.18) | copy-start | bytes 3145732
  253.8 6.2 %copy-start.4 = (f32[8,32,32,32]{3,2,1,0:T(8,128)S(1)}, f32[8,32,32,32]{3,2,1,0:T(8,128)}, u32[]{:S(2)}) copy-start(f32[8,32,32,32]{3,2,1,0:T(8,128)} %reshape.226) | copy-start | bytes 3145732
  333.4 45.4 %copy-start.15 = (f32[2,2,2,2,1,1]{1,2,3,0,5,4:T(2,128)S(1)}, f32[2,2,2,2,1,1]{1,2,3,0,5,4:T(2,128)}, u32[]{:S(2)}) copy-start(f32[2,2,2,2,1,1]{1,2,3,0,5,4:T(2,128)} %copy.192) | copy-start | bytes 196
  413.7 7.8 %copy-start.21 = (u32[32]{0:T(128)S(1)}, u32[32]{0:T(128)}, u32[]{:S(2)}) copy-start(u32[32]{0:T(128)} %constant.101) | copy-start | bytes 388
  413.7 8.4 %copy-start.20 = (s32[8]{0:T(128)S(1)}, s32[8]{0:T(128)}, u32[]{:S(2)}) copy-start(s32[8]{0:T(128)} %param.17) | copy-start | bytes 100
Sparse Core Ops, SparseCore 0:
  421.6 17.0 all-reduce.2
